TPU v7x, 32 devices: a whole 2x2x4 slice. The times are simulated.
32 devices in a mesh: groups: 2 (over y), fsdp: 8 (over z, x), rep: 2 (over core).
Axes of the slice: x: 2, y: 2, z: 4, core: 2. Of those that a mesh axis runs over, the one named last changes fastest.
Arguments:
- weights: bfloat16 [448, 128, 1024], P(('groups', 'fsdp'), None, 'rep'), parts along dimension 0
- block_ids: int32 [224], replicated, may hold values from 0 to 223, as said below
- owner_map: int32 [8], replicated, may hold values from 0 to 7, each once
Outputs:
- quantized: bfloat16 [16, 1024, 3584], P(('groups', 'fsdp')), parts along dimension 0
- scales: bfloat16 [16, 8, 28], P(('groups', 'fsdp')), parts along dimension 0
There are 2 independent parts, one for each index of `groups`. A program takes and returns all parts, laid end to end along the dimension named above; an argument that names none is the same for every part. Nothing has to cross between parts.
Inputs may be any that keep to these rules, and one draw needn't show every extreme that they name: block_ids names every one of the 224 blocks once; each device's 28 slots hold one block of each block row j, and at most 4 blocks of any one expert, a number that some device reaches. `owner_map`: every device along fsdp owns exactly one expert.
All inputs are finite; a program needn't handle non-finite values.
Results may differ from a plain program's by a relative error of at most 0.001.
Values may be sent and summed in bfloat16 or wider, within the bound.
A program may use at most 128 MiB of HBM per device.

v0:
```python
import jax
import jax.numpy as jnp
from jax import lax
from jax.sharding import PartitionSpec as P


def quantize(blocks):
    amount, height, breadth = blocks.shape
    widened = blocks.astype(jnp.float32).reshape(amount, height, breadth // 128, 128)
    largest = jnp.max(jnp.abs(widened), axis=(1, 3))
    block_scale = (largest + 1e-06).astype(jnp.bfloat16)
    divided = widened / block_scale.astype(jnp.float32)[:, None, :, None]
    return (divided.astype(jnp.bfloat16).reshape(amount, height, breadth), block_scale)


def body(weights, block_ids, owner_map):
    shards = lax.axis_size("fsdp")
    myself = lax.axis_index("fsdp")
    per_device = block_ids.shape[0] // shards
    experts_total = owner_map.shape[0]
    capacity = (per_device + shards - 1) // shards
    layout = block_ids.reshape(shards, per_device)
    expert_ids = jnp.arange(experts_total, dtype=jnp.int32)
    holder = layout // per_device
    target_owner = jnp.sum(jnp.where(holder[:, :, None] == expert_ids, owner_map, 0), axis=2)
    local_ids = jnp.arange(per_device, dtype=jnp.int32)
    same_owner = target_owner[:, :, None] == target_owner[:, None, :]
    earlier = local_ids[None, None, :] < local_ids[None, :, None]
    ranking = jnp.sum(jnp.where(same_owner & earlier, 1, 0), axis=2)
    position = target_owner * capacity + ranking
    my_position = lax.dynamic_index_in_dim(position, myself, 0, keepdims=False)
    places = jnp.arange(shards * capacity, dtype=jnp.int32)
    hitting = my_position[None, :] == places[:, None]
    source = jnp.sum(jnp.where(hitting, local_ids[None, :], 0), axis=1)
    present = jnp.any(hitting, axis=1)
    my_expert = jnp.sum(jnp.where(owner_map == myself, expert_ids, 0))
    wanted = my_expert * per_device + local_ids
    matches = layout[None, :, :] == wanted[:, None, None]
    received_at = jnp.arange(shards, dtype=jnp.int32)[:, None] * capacity + ranking
    picking = jnp.sum(jnp.where(matches, received_at[None], 0), axis=(1, 2))
    full_columns = lax.all_gather(weights, "rep", axis=2, tiled=True)
    scaled, block_scale = quantize(full_columns)
    payload = jnp.where(present[:, None, None], scaled[source], jnp.zeros((), scaled.dtype))
    scale_tiles = jnp.where(present[:, None], block_scale[source], jnp.zeros((), block_scale.dtype))
    payload = payload.reshape(shards, capacity, scaled.shape[1], scaled.shape[2])
    scale_tiles = scale_tiles.reshape(shards, capacity, block_scale.shape[1])
    payload, scale_tiles = (payload, scale_tiles)
    payload, scale_tiles = (
        lax.all_to_all(payload, "fsdp", split_axis=0, concat_axis=0, tiled=True),
        lax.all_to_all(scale_tiles, "fsdp", split_axis=0, concat_axis=0, tiled=True),
    )
    flat_blocks = payload.reshape(shards * capacity, payload.shape[2], payload.shape[3])[picking]
    flat_scales = scale_tiles.reshape(shards * capacity, scale_tiles.shape[2])[picking]
    matrix = flat_blocks.reshape(per_device * payload.shape[2], payload.shape[3]).T
    matrix, scale_rows = (matrix, flat_scales.T)
    return (matrix[None], scale_rows[None])


def solution(mesh):
    return jax.shard_map(
        body,
        mesh=mesh,
        in_specs=(P(("groups", "fsdp"), None, "rep"), P(), P()),
        out_specs=(P(("groups", "fsdp"), None, None), P(("groups", "fsdp"), None, None)),
        check_vma=False,
    )
```

profile of v0, /device:TPU:11, one launch (start us, length us, event | category | flops | bytes accessed | tf_op | source)
XLA Modules:
  0.0 276.8 jit_solution(4032116689433841013)
XLA Ops:
  7.2 0.0 all-gather.2.cloned.1.call-start
  7.2 0.7 all-gather.2.cloned.1.call-update
  7.9 0.8 reshape.124
  8.7 0.7 select_reduce_fusion.2
  9.4 0.1 copy.13
  9.5 0.6 select_reduce_fusion.1
  10.1 0.1 copy.14
  10.2 0.1 broadcast_add_fusion
  10.3 0.1 fusion.2
  10.4 0.1 broadcast_in_dim.99
  10.5 0.1 select_reduce_fusion.3
  10.7 19.1 %all-gather.2.cloned.1.call-done = bf16[28,128,1024]{2,1,0:T(8,128)(2,1)} async-done(((bf16[28,128,512]{2,1,0:T(8,128)(2,1)}), bf16[28,128,1024]{2,1,0:T(8,128)(2,1)}) %all-gather.2.cloned.1.call-update) | async-done | bytes 7340048 | tf_op jit(solution)/shard_map/all_gather | solution.py:41
  29.8 5.1 %fusion = f32[28,1024]{1,0:T(8,128)S(1)} fusion(bf16[28,128,1024]{2,1,0:T(8,128)(2,1)} %all-gather.2.cloned.1.call-done), kind=kLoop, calls=%fused_computation.6 | loop fusion | flops 10981376 | bytes 7454720 | tf_op jit(solution)/shard_map/reduce_max | solution.py:10
  34.9 0.1 slice_reduce_fusion
  35.0 0.6 gather_fusion.2
  35.6 0.7 broadcast_select_fusion.1
  36.3 5.5 %all-to-all-start.1 = ((bf16[8,4,8]{2,1,0:T(4,128)(2,1)}), bf16[8,4,8]{2,1,0:T(4,128)(2,1)S(1)}, u32[]{:S(2)}, u32[]{:S(2)}) async-start(bf16[8,4,8]{2,1,0:T(4,128)(2,1)} %broadcast_select_fusion.1), calls=%async_computation.1 | async-start | bytes 16384 | tf_op jit(solution)/shard_map/all_to_all | solution.py:50
  41.8 0.1 div.24
  41.9 8.6 %fusion.1 = bf16[28,128,1024]{2,1,0:T(8,128)(2,1)} fusion(bf16[28,128,1024]{2,1,0:T(8,128)(2,1)} %all-gather.2.cloned.1.call-done, f32[28,1024]{1,0:T(8,128)S(1)} %bitcast.31), kind=kLoop, calls=%fused_computation.7 | loop fusion | flops 11010048 | bytes 14794752 | tf_op jit(solution)/shard_map/convert_element_type | solution.py:13
  50.5 8.1 %gather_fusion = bf16[32,128,1024]{2,1,0:T(8,128)(2,1)} fusion(bf16[28,128,1024]{2,1,0:T(8,128)(2,1)} %fusion.1, s32[1024]{0:T(1024)S(1)} %pad_clamp_fusion.1), kind=kCustom, calls=%fused_computation | custom fusion | bytes 16777344 | tf_op jit(solution)/shard_map/gather | solution.py:43
  58.6 7.2 %broadcast_select_fusion = bf16[8,4,128,1024]{3,2,1,0:T(8,128)(2,1)} fusion(bf16[8,4,128,1024]{3,2,1,0:T(8,128)(2,1)} %bitcast.28, pred[8,4]{1,0:T(8,128)(4,1)S(1)} %broadcast_in_dim.99), kind=kLoop, calls=%fused_computation.8 | loop fusion | flops 4194304 | bytes 16777248 | tf_op jit(solution)/shard_map/jit(_where)/select_n | solution.py:43
  65.8 0.0 copy-start
  65.8 0.0 all-to-all-done.1
  65.8 5.6 %all-to-all-start = ((bf16[8,4,128,1024]{3,2,1,0:T(8,128)(2,1)}), bf16[8,4,128,1024]{3,2,1,0:T(8,128)(2,1)}, u32[]{:S(2)}, u32[]{:S(2)}) async-start(bf16[8,4,128,1024]{3,2,1,0:T(8,128)(2,1)} %broadcast_select_fusion), calls=%async_computation | async-start | bytes 16777216 | tf_op jit(solution)/shard_map/all_to_all | solution.py:49
  71.4 0.0 copy-done
  71.4 0.6 fusion.4
  72.7 0.7 select_reduce_fusion
  73.4 0.6 gather_fusion.3
  73.9 0.7 copy.17
  74.6 177.3 %all-to-all-done = bf16[8,4,128,1024]{3,2,1,0:T(8,128)(2,1)} async-done(((bf16[8,4,128,1024]{3,2,1,0:T(8,128)(2,1)}), bf16[8,4,128,1024]{3,2,1,0:T(8,128)(2,1)}, u32[]{:S(2)}, u32[]{:S(2)}) %all-to-all-start) | async-done | bytes 8388640 | tf_op jit(solution)/shard_map/all_to_all | solution.py:49
  251.9 8.1 %gather_fusion.1 = bf16[28,128,1024]{2,1,0:T(8,128)(2,1)} fusion(bf16[32,128,1024]{2,1,0:T(8,128)(2,1)} %bitcast.4, s32[1024]{0:T(1024)S(1)} %pad_clamp_fusion), kind=kCustom, calls=%fused_computation.1 | custom fusion | bytes 14680176 | tf_op jit(solution)/shard_map/gather | solution.py:52
  260.1 9.9 %copy.16 = bf16[1,1024,3584]{2,1,0:T(8,128)(2,1)} copy(bf16[1,1024,3584]{1,2,0:T(8,128)(2,1)} %bitcast.29) | data formatting | bytes 14680064
  (13 shorter events, 0.1 us)
Async XLA Ops:
  7.2 22.6 %all-gather.2.cloned.1.call-start = ((), (), s32[]{:S(2)}) async-start(), calls=%async_computation.2 | async-start | bytes 11010048 | tf_op jit(solution)/shard_map/all_gather | solution.py:41
  36.3 29.5 %all-to-all-start.1 = ((bf16[8,4,8]{2,1,0:T(4,128)(2,1)}), bf16[8,4,8]{2,1,0:T(4,128)(2,1)S(1)}, u32[]{:S(2)}, u32[]{:S(2)}) async-start(bf16[8,4,8]{2,1,0:T(4,128)(2,1)} %broadcast_select_fusion.1), calls=%async_computation.1 | async-start | bytes 16384 | tf_op jit(solution)/shard_map/all_to_all | solution.py:50
  65.8 5.6 %copy-start = (s32[8]{0:T(128)S(1)}, s32[8]{0:T(128)}, u32[]{:S(2)}) copy-start(s32[8]{0:T(128)} %param.5) | copy-start | bytes 100
  65.8 186.1 %all-to-all-start = ((bf16[8,4,128,1024]{3,2,1,0:T(8,128)(2,1)}), bf16[8,4,128,1024]{3,2,1,0:T(8,128)(2,1)}, u32[]{:S(2)}, u32[]{:S(2)}) async-start(bf16[8,4,128,1024]{3,2,1,0:T(8,128)(2,1)} %broadcast_select_fusion), calls=%async_computation | async-start | bytes 16777216 | tf_op jit(solution)/shard_map/all_to_all | solution.py:49
Sparse Core Ops, SparseCore 0:
  9.5 20.1 all-gather.1
where the time goes:
time: 282 us; the launch traced here: 277 us
  waiting for transfers between devices  197 us (70%)
  local copies, waits for them, and re-layouts  29.2 us (10%)
  other arithmetic  24.7 us (9%)
  between operations  14.8 us (5%)
  starting transfers between devices  11.1 us (4%)
    all_to_all x1, waiting for transfers between devices, body(): lax.all_to_all(payload, 'fsdp', split_axis=0, concat_axis=0, tiled=True)  177 us
    all_gather x1, waiting for transfers between devices, body(): full_columns = lax.all_gather(weights, 'rep', axis=2, tiled=True)  19.1 us
    unnamed x7, local copies, waits for them, and re-layouts  10.7 us
    convert_element_type x1, other arithmetic, quantize(): divided.astype(jnp.bfloat16).reshape(amount, height, breadth)  8.58 us
    gather x1, local copies, waits for them, and re-layouts, body(): payload.reshape(shards * capacity, payload.shape[2], payload.shape[3])  8.14 us
    gather x1, local copies, waits for them, and re-layouts, body(): scaled[source]  8.07 us
    select_n x1, other arithmetic, body(): jnp.where(present[:, None, None], scaled[source], jnp.zeros((), scaled.dt...  7.22 us
  transfers between devices with their start and end apart: 3, of which 2 were waited for; matrix products, arithmetic and copies ran while one was open for 11% of the time, Pallas kernels for 0%

commit v1 on v0

v1 whole, which is shorter than its diff:
```python
import functools

import jax
import jax.numpy as jnp
from jax import lax
from jax.experimental import pallas as pl
from jax.experimental.pallas import tpu as pltpu
from jax.sharding import PartitionSpec as P

MESH = pl.DeviceIdType.MESH
LANES = 128


def far_first(step, shards):
    distance = (step + 1) // 2
    sign = 1 - 2 * ((step + 1) % 2)
    return (shards // 2 + sign * distance + shards) % shards


def exchange_kernel(
    shards, capacity, source_ref, weights_ref, landed_ref, outgoing, send_sem, recv_sem, pass_sem, passed_sem
):
    me = lax.axis_index("fsdp")
    core = lax.axis_index("rep")
    other = 1 - core
    columns = weights_ref.shape[2]
    tiles = columns // LANES
    block_rows = capacity * columns

    barrier = pltpu.get_barrier_semaphore()

    def greet(step, carry):
        peer = (me + step) % shards
        pl.semaphore_signal(barrier, inc=1, device_id={"fsdp": peer}, device_id_type=MESH)
        return carry

    lax.fori_loop(1, shards, greet, 0)
    pl.semaphore_signal(barrier, inc=1, device_id={"rep": other}, device_id_type=MESH)
    pl.semaphore_wait(barrier, shards)

    def fill(owner):
        scale_rows = outgoing.shape[1] - block_rows
        row_ids = lax.broadcasted_iota(jnp.int32, (scale_rows, LANES), 0)
        scale_tile = jnp.zeros((scale_rows, LANES), jnp.float32)
        for slot in range(capacity):
            source = source_ref[owner * capacity + slot]
            for tile in range(tiles):
                block = weights_ref[source, :, tile * LANES : (tile + 1) * LANES].astype(jnp.float32)
                largest = jnp.max(jnp.max(jnp.abs(block), axis=0, keepdims=True), axis=1, keepdims=True)
                scale = (largest + 1e-06).astype(jnp.bfloat16).astype(jnp.float32)
                divided = (block / scale).astype(jnp.bfloat16)
                start = (slot * tiles + tile) * LANES
                outgoing[owner, start : start + LANES, :] = divided.T
                scale_tile = jnp.where(row_ids == slot * tiles + tile, scale, scale_tile)
        outgoing[owner, block_rows:, :] = scale_tile.astype(jnp.bfloat16)

    def to_owner(owner):
        return pltpu.make_async_remote_copy(
            src_ref=outgoing.at[owner],
            dst_ref=landed_ref.at[core, me],
            send_sem=send_sem.at[owner],
            recv_sem=recv_sem.at[me],
            device_id={"fsdp": owner},
            device_id_type=MESH,
        )

    def from_sender(sender):
        return pltpu.make_async_remote_copy(
            src_ref=outgoing.at[sender],
            dst_ref=landed_ref.at[core, sender],
            send_sem=send_sem.at[sender],
            recv_sem=recv_sem.at[sender],
            device_id={"fsdp": sender},
            device_id_type=MESH,
        )

    def to_core(sender):
        return pltpu.make_async_remote_copy(
            src_ref=landed_ref.at[core, sender],
            dst_ref=landed_ref.at[core, sender],
            send_sem=pass_sem.at[sender],
            recv_sem=passed_sem.at[sender],
            device_id={"rep": other},
            device_id_type=MESH,
        )

    def from_core(sender):
        return pltpu.make_async_remote_copy(
            src_ref=landed_ref.at[other, sender],
            dst_ref=landed_ref.at[other, sender],
            send_sem=pass_sem.at[sender],
            recv_sem=passed_sem.at[sender],
            device_id={"rep": other},
            device_id_type=MESH,
        )

    def send(step, carry):
        owner = (me + far_first(step, shards)) % shards
        fill(owner)
        to_owner(owner).start()
        return carry

    lax.fori_loop(0, shards - 1, send, 0)
    fill(me)
    keep = pltpu.make_async_copy(outgoing.at[me], landed_ref.at[core, me], recv_sem.at[me])
    keep.start()
    keep.wait()
    to_core(me).start()

    def forward(step, carry):
        sender = (me - far_first(step, shards) + shards) % shards
        from_sender(sender).wait_recv()
        to_core(sender).start()
        return carry

    lax.fori_loop(0, shards - 1, forward, 0)

    def finish(step, carry):
        peer = (me + step) % shards
        to_owner(peer).wait_send()
        return carry

    lax.fori_loop(1, shards, finish, 0)

    def finish_core(sender, carry):
        to_core(sender).wait_send()
        from_core(sender).wait_recv()
        return carry

    lax.fori_loop(0, shards, finish_core, 0)


def place_kernel(capacity, columns, pick_ref, landed_ref, matrix_ref, scales_ref, scale_tiles, scale_sem, sems):
    cores, shards, rows, _ = landed_ref.shape
    per_device = pick_ref.shape[0]
    tiles = columns // LANES
    block_rows = capacity * columns
    scale_copy = pltpu.make_async_copy(
        landed_ref.at[:, :, pl.ds(block_rows, rows - block_rows), :], scale_tiles, scale_sem
    )
    scale_copy.start()

    def move(index, half):
        picked = pick_ref[index]
        sender, slot = picked // capacity, picked % capacity
        return pltpu.make_async_copy(
            landed_ref.at[half, sender, pl.ds(pl.multiple_of(slot * columns, columns), columns), :],
            matrix_ref.at[0, pl.ds(half * columns, columns), pl.ds(pl.multiple_of(index * LANES, LANES), LANES)],
            sems.at[half, index],
        )

    def begin(index, carry):
        for half in range(cores):
            move(index, half).start()
        return carry

    lax.fori_loop(0, per_device, begin, 0)
    scale_copy.wait()
    lanes = lax.broadcasted_iota(jnp.int32, (rows - block_rows, LANES), 1)
    rows_of = lax.broadcasted_iota(jnp.int32, (rows - block_rows, LANES), 0)

    def gather(index, totals):
        picked = pick_ref[index]
        sender, slot = picked // capacity, picked % capacity
        hit = (lanes == index) & (rows_of // tiles == slot)
        return tuple(
            jnp.where(hit, scale_tiles[half, sender].astype(jnp.float32), totals[half]) for half in range(cores)
        )

    zero = jnp.zeros((rows - block_rows, LANES), jnp.float32)
    totals = lax.fori_loop(0, per_device, gather, (zero,) * cores)
    for half in range(cores):
        folded = jnp.zeros((tiles, LANES), jnp.float32)
        for slot in range(capacity):
            folded = folded + totals[half][slot * tiles : (slot + 1) * tiles]
        scales_ref[0, half * tiles : (half + 1) * tiles, :] = folded[:, :per_device].astype(jnp.bfloat16)

    def end(index, carry):
        for half in range(cores):
            move(index, half).wait()
        return carry

    lax.fori_loop(0, per_device, end, 0)


def body(weights, block_ids, owner_map):
    shards = lax.axis_size("fsdp")
    cores = lax.axis_size("rep")
    myself = lax.axis_index("fsdp")
    per_device, height, columns = weights.shape
    experts_total = owner_map.shape[0]
    capacity = (per_device + shards - 1) // shards
    layout = block_ids.reshape(shards, per_device)
    expert_ids = jnp.arange(experts_total, dtype=jnp.int32)
    local_ids = jnp.arange(per_device, dtype=jnp.int32)
    holder = layout // per_device
    earlier = local_ids[None, :] < local_ids[:, None]

    mine = lax.dynamic_index_in_dim(holder, myself, 0, keepdims=False)
    my_owner = jnp.sum(jnp.where(mine[:, None] == expert_ids, owner_map, 0), axis=1)
    my_rank = jnp.sum(jnp.where((mine[:, None] == mine[None, :]) & earlier, 1, 0), axis=1)
    places = jnp.arange(shards * capacity, dtype=jnp.int32)
    source = jnp.sum(jnp.where((my_owner * capacity + my_rank)[None, :] == places[:, None], local_ids[None, :], 0), axis=1)

    my_expert = jnp.sum(jnp.where(owner_map == myself, expert_ids, 0))
    held = holder == my_expert
    ranking = jnp.sum(jnp.where(held[:, None, :] & earlier[None], 1, 0), axis=2)
    received_at = jnp.arange(shards, dtype=jnp.int32)[:, None] * capacity + ranking
    matches = layout[None, :, :] == (my_expert * per_device + local_ids)[:, None, None]
    picking = jnp.sum(jnp.where(matches, received_at[None], 0), axis=(1, 2))

    tiles = columns // LANES
    scale_rows = (capacity * tiles + 15) // 16 * 16
    rows = capacity * columns + scale_rows
    landed = pl.pallas_call(
        functools.partial(exchange_kernel, shards, capacity),
        out_shape=jax.ShapeDtypeStruct((cores, shards, rows, LANES), jnp.bfloat16),
        in_specs=[pl.BlockSpec(memory_space=pltpu.SMEM), pl.BlockSpec(memory_space=pltpu.VMEM)],
        out_specs=pl.BlockSpec(memory_space=pl.ANY),
        scratch_shapes=[
            pltpu.VMEM((shards, rows, LANES), jnp.bfloat16),
            pltpu.SemaphoreType.DMA((shards,)),
            pltpu.SemaphoreType.DMA((shards,)),
            pltpu.SemaphoreType.DMA((shards,)),
            pltpu.SemaphoreType.DMA((shards,)),
        ],
        compiler_params=pltpu.CompilerParams(
            collective_id=0, has_side_effects=True, vmem_limit_bytes=48 * 1024 * 1024
        ),
        name="exchange",
    )(source, weights)
    return pl.pallas_call(
        functools.partial(place_kernel, capacity, columns),
        out_shape=(
            jax.ShapeDtypeStruct((1, cores * columns, per_device * height), jnp.bfloat16),
            jax.ShapeDtypeStruct((1, cores * tiles, per_device), jnp.bfloat16),
        ),
        in_specs=[pl.BlockSpec(memory_space=pltpu.SMEM), pl.BlockSpec(memory_space=pl.ANY)],
        out_specs=(pl.BlockSpec(memory_space=pl.ANY), pl.BlockSpec(memory_space=pltpu.VMEM)),
        scratch_shapes=[
            pltpu.VMEM((cores, shards, scale_rows, LANES), jnp.bfloat16),
            pltpu.SemaphoreType.DMA,
            pltpu.SemaphoreType.DMA((cores, per_device)),
        ],
        compiler_params=pltpu.CompilerParams(vmem_limit_bytes=48 * 1024 * 1024),
        name="place",
    )(picking, landed)


def solution(mesh):
    return jax.shard_map(
        body,
        mesh=mesh,
        in_specs=(P(("groups", "fsdp"), None, "rep"), P(), P()),
        out_specs=(P(("groups", "fsdp"), None, None), P(("groups", "fsdp"), None, None)),
        check_vma=False,
    )
```

time: 282 us -> 334 us (1.18); the launches traced: 277 us -> 334 us
  Pallas kernels: 0 us -> 325 us
  waiting for transfers between devices: 197 us -> 0 us
  local copies, waits for them, and re-layouts: 29.2 us -> 2.88 us
  other arithmetic: 24.7 us -> 4.31 us
  between operations: 14.8 us -> 1.34 us
  starting transfers between devices: 11.1 us -> 0 us
    pallas_call x0 -> x2, Pallas kernels: none -> 325 us  [the longest x1 225 us: body(): pl.pallas_call(functools.partial(place_kernel, capacity, columns), out_sh...]
    all_to_all x2 -> x0, waiting for transfers between devices: 177 us -> none  [the longest x1 177 us: body(): lax.all_to_all(payload, 'fsdp', split_axis=0, concat_axis=0, tiled=True)]
    all_gather x1 -> x0, waiting for transfers between devices: 19.1 us -> none  [body(): full_columns = lax.all_gather(weights, 'rep', axis=2, tiled=True)]
    gather x4 -> x0, local copies, waits for them, and re-layouts: 17.4 us -> none  [the longest x1 8.14 us: body(): payload.reshape(shards * capacity, payload.shape[2], payload.shape[3])]
    all_to_all x2 -> x0, starting transfers between devices: 11.1 us -> none  [the longest x1 5.57 us: body(): lax.all_to_all(payload, 'fsdp', split_axis=0, concat_axis=0, tiled=True)]
    unnamed x7 -> x2, local copies, waits for them, and re-layouts: 10.7 us -> 2.04 us
    convert_element_type x2 -> x0, other arithmetic: 8.59 us -> none  [the longest x1 8.58 us: quantize(): divided.astype(jnp.bfloat16).reshape(amount, height, breadth)]
    select_n x5 -> x0, other arithmetic: 7.92 us -> none  [the longest x1 7.22 us: body(): jnp.where(present[:, None, None], scaled[source], jnp.zeros((), scaled.dt...]
  transfers between devices with their start and end apart: 3 -> 0, of which waited for: 2 -> 0; matrix products, arithmetic and copies ran while one was open for 11% -> 0% of each run, Pallas kernels for 0% -> 0%
where the time goes in v1:
time: 334 us
  Pallas kernels  325 us (97%)
  other arithmetic  4.31 us (1%)
    pallas_call x1, Pallas kernels, body(): pl.pallas_call(functools.partial(place_kernel, capacity, columns), out_sh...  225 us
    pallas_call x1, Pallas kernels, body(): pl.pallas_call(functools.partial(exchange_kernel, shards, capacity), out_...  100 us

profile of v1, /device:TPU:11, one launch (start us, length us, event | category | flops | bytes accessed | tf_op | source)
XLA Modules:
  0.0 333.9 jit_solution(9966966594635842757)
XLA Ops:
  0.6 1.3 fusion.1
  2.6 0.8 eq.72
  3.4 0.7 broadcast_compare_fusion
  4.1 0.2 select_reduce_fusion.3
  4.2 0.7 select_reduce_fusion.4
  5.0 0.1 select_reduce_fusion.2.source_ref
  5.1 0.6 select_reduce_fusion.1
  5.7 0.1 copy.6
  5.7 0.1 broadcast_add_fusion
  5.8 0.7 select_reduce_fusion.pick_ref
  6.5 0.0 copy-start
  6.5 2.0 copy-done
  8.5 100.3 %exchange.1.landed_ref = bf16[2,8,2064,128]{3,2,1,0:T(8,128)(2,1)} custom-call(s32[32]{0:T(128)S(1)} %select_reduce_fusion.2.source_ref, bf16[28,128,512]{2,1,0:T(8,128)(2,1)S(1)} %copy-done), custom_call_target="tpu_custom_call" | custom-call | tf_op jit(solution)/shard_map/exchange/pallas_call | solution.py:215
  108.8 225.1 %place.1 = (bf16[1,1024,3584]{2,1,0:T(8,128)(2,1)}, bf16[1,8,28]{2,1,0:T(8,128)(2,1)}) custom-call(s32[28]{0:T(128)S(1)} %select_reduce_fusion.pick_ref, bf16[2,8,2064,128]{3,2,1,0:T(8,128)(2,1)} %exchange.1.landed_ref), custom_call_target="tpu_custom_call" | custom-call | tf_op jit(solution)/shard_map/place/pallas_call | solution.py:232
  (5 shorter events, 0.0 us)
Async XLA Ops:
  6.5 2.0 copy-start

commit v2 on v1

--- a/solution.py
+++ b/solution.py
@@ -18,14 +18,29 @@
 
 
 def exchange_kernel(
-    shards, capacity, source_ref, weights_ref, landed_ref, outgoing, send_sem, recv_sem, pass_sem, passed_sem
+    shards,
+    capacity,
+    block_ids_ref,
+    owner_map_ref,
+    weights_ref,
+    landed_ref,
+    held_weights,
+    outgoing,
+    owner_of,
+    read_sem,
+    send_sem,
+    recv_sem,
+    pass_sem,
+    passed_sem,
 ):
     me = lax.axis_index("fsdp")
     core = lax.axis_index("rep")
     other = 1 - core
-    columns = weights_ref.shape[2]
+    per_device, _, columns = weights_ref.shape
     tiles = columns // LANES
     block_rows = capacity * columns
+    read = pltpu.make_async_copy(weights_ref, held_weights, read_sem)
+    read.start()
 
     barrier = pltpu.get_barrier_semaphore()
 
@@ -36,20 +51,38 @@
 
     lax.fori_loop(1, shards, greet, 0)
     pl.semaphore_signal(barrier, inc=1, device_id={"rep": other}, device_id_type=MESH)
+
+    def look_up(index, carry):
+        owner_of[index] = owner_map_ref[lax.div(block_ids_ref[me * per_device + index], per_device)]
+        return carry
+
+    lax.fori_loop(0, per_device, look_up, 0)
     pl.semaphore_wait(barrier, shards)
+    read.wait()
+
+    def sources_for(owner):
+        def step(index, carry):
+            count, found = carry
+            hit = owner_of[index] == owner
+            found = tuple(jnp.where(hit & (count == slot), index, old) for slot, old in enumerate(found))
+            return count + hit.astype(jnp.int32), found
+
+        zero = jnp.int32(0)
+        return lax.fori_loop(0, per_device, step, (zero, (zero,) * capacity))[1]
 
     def fill(owner):
+        sources = sources_for(owner)
         scale_rows = outgoing.shape[1] - block_rows
         row_ids = lax.broadcasted_iota(jnp.int32, (scale_rows, LANES), 0)
         scale_tile = jnp.zeros((scale_rows, LANES), jnp.float32)
         for slot in range(capacity):
-            source = source_ref[owner * capacity + slot]
+            source = sources[slot]
             for tile in range(tiles):
-                block = weights_ref[source, :, tile * LANES : (tile + 1) * LANES].astype(jnp.float32)
+                block = held_weights[source, :, tile * LANES : (tile + 1) * LANES].astype(jnp.float32)
                 largest = jnp.max(jnp.max(jnp.abs(block), axis=0, keepdims=True), axis=1, keepdims=True)
                 scale = (largest + 1e-06).astype(jnp.bfloat16).astype(jnp.float32)
                 divided = (block / scale).astype(jnp.bfloat16)
-                start = (slot * tiles + tile) * LANES
+                start = (tile * capacity + slot) * LANES
                 outgoing[owner, start : start + LANES, :] = divided.T
                 scale_tile = jnp.where(row_ids == slot * tiles + tile, scale, scale_tile)
         outgoing[owner, block_rows:, :] = scale_tile.astype(jnp.bfloat16)
@@ -130,38 +163,80 @@
     lax.fori_loop(0, shards, finish_core, 0)
 
 
-def place_kernel(capacity, columns, pick_ref, landed_ref, matrix_ref, scales_ref, scale_tiles, scale_sem, sems):
+def place_kernel(
+    capacity,
+    columns,
+    block_ids_ref,
+    owner_map_ref,
+    landed_ref,
+    matrix_ref,
+    scales_ref,
+    pieces,
+    staged,
+    scale_tiles,
+    pick_ref,
+    read_sems,
+    write_sems,
+    scale_sem,
+):
+    me = lax.axis_index("fsdp")
     cores, shards, rows, _ = landed_ref.shape
-    per_device = pick_ref.shape[0]
+    per_device = pick_ref.shape[0] - 1
     tiles = columns // LANES
     block_rows = capacity * columns
+    piece_rows = capacity * LANES
+
+    def read(piece):
+        half, tile = piece // tiles, piece % tiles
+        return pltpu.make_async_copy(
+            landed_ref.at[half, :, pl.ds(tile * piece_rows, piece_rows), :], pieces.at[piece], read_sems.at[piece]
+        )
+
+    def write(piece):
+        return pltpu.make_async_copy(
+            staged.at[piece], matrix_ref.at[0, pl.ds(piece * LANES, LANES), :], write_sems.at[piece]
+        )
+
     scale_copy = pltpu.make_async_copy(
         landed_ref.at[:, :, pl.ds(block_rows, rows - block_rows), :], scale_tiles, scale_sem
     )
+    for piece in range(cores * tiles):
+        read(piece).start()
     scale_copy.start()
 
-    def move(index, half):
-        picked = pick_ref[index]
-        sender, slot = picked // capacity, picked % capacity
-        return pltpu.make_async_copy(
-            landed_ref.at[half, sender, pl.ds(pl.multiple_of(slot * columns, columns), columns), :],
-            matrix_ref.at[0, pl.ds(half * columns, columns), pl.ds(pl.multiple_of(index * LANES, LANES), LANES)],
-            sems.at[half, index],
-        )
-
-    def begin(index, carry):
-        for half in range(cores):
-            move(index, half).start()
-        return carry
-
-    lax.fori_loop(0, per_device, begin, 0)
+    def find_expert(expert, found):
+        return jnp.where(owner_map_ref[expert] == me, expert, found)
+
+    lowest = per_device * lax.fori_loop(0, owner_map_ref.shape[0], find_expert, jnp.int32(0))
+
+    def look_up(sender, carry):
+        count = jnp.int32(0)
+        for index in range(per_device):
+            row = block_ids_ref[sender * per_device + index] - lowest
+            hit = (row >= 0) & (row < per_device)
+            pick_ref[jnp.where(hit, row, per_device)] = sender * capacity + count
+            count = count + hit.astype(jnp.int32)
+        return carry
+
+    lax.fori_loop(0, shards, look_up, 0)
+
+    for piece in range(cores * tiles):
+        read(piece).wait()
+
+        for index in range(per_device):
+            picked = pick_ref[index]
+            sender, slot = lax.div(picked, capacity), lax.rem(picked, capacity)
+            staged[piece, :, index * LANES : (index + 1) * LANES] = pieces[
+                piece, sender, pl.ds(pl.multiple_of(slot * LANES, LANES), LANES), :
+            ]
+        write(piece).start()
     scale_copy.wait()
     lanes = lax.broadcasted_iota(jnp.int32, (rows - block_rows, LANES), 1)
     rows_of = lax.broadcasted_iota(jnp.int32, (rows - block_rows, LANES), 0)
 
     def gather(index, totals):
         picked = pick_ref[index]
-        sender, slot = picked // capacity, picked % capacity
+        sender, slot = lax.div(picked, capacity), lax.rem(picked, capacity)
         hit = (lanes == index) & (rows_of // tiles == slot)
         return tuple(
             jnp.where(hit, scale_tiles[half, sender].astype(jnp.float32), totals[half]) for half in range(cores)
@@ -175,50 +250,29 @@
             folded = folded + totals[half][slot * tiles : (slot + 1) * tiles]
         scales_ref[0, half * tiles : (half + 1) * tiles, :] = folded[:, :per_device].astype(jnp.bfloat16)
 
-    def end(index, carry):
-        for half in range(cores):
-            move(index, half).wait()
-        return carry
-
-    lax.fori_loop(0, per_device, end, 0)
+    for piece in range(cores * tiles):
+        write(piece).wait()
 
 
 def body(weights, block_ids, owner_map):
     shards = lax.axis_size("fsdp")
     cores = lax.axis_size("rep")
-    myself = lax.axis_index("fsdp")
     per_device, height, columns = weights.shape
-    experts_total = owner_map.shape[0]
     capacity = (per_device + shards - 1) // shards
-    layout = block_ids.reshape(shards, per_device)
-    expert_ids = jnp.arange(experts_total, dtype=jnp.int32)
-    local_ids = jnp.arange(per_device, dtype=jnp.int32)
-    holder = layout // per_device
-    earlier = local_ids[None, :] < local_ids[:, None]
-
-    mine = lax.dynamic_index_in_dim(holder, myself, 0, keepdims=False)
-    my_owner = jnp.sum(jnp.where(mine[:, None] == expert_ids, owner_map, 0), axis=1)
-    my_rank = jnp.sum(jnp.where((mine[:, None] == mine[None, :]) & earlier, 1, 0), axis=1)
-    places = jnp.arange(shards * capacity, dtype=jnp.int32)
-    source = jnp.sum(jnp.where((my_owner * capacity + my_rank)[None, :] == places[:, None], local_ids[None, :], 0), axis=1)
-
-    my_expert = jnp.sum(jnp.where(owner_map == myself, expert_ids, 0))
-    held = holder == my_expert
-    ranking = jnp.sum(jnp.where(held[:, None, :] & earlier[None], 1, 0), axis=2)
-    received_at = jnp.arange(shards, dtype=jnp.int32)[:, None] * capacity + ranking
-    matches = layout[None, :, :] == (my_expert * per_device + local_ids)[:, None, None]
-    picking = jnp.sum(jnp.where(matches, received_at[None], 0), axis=(1, 2))
-
     tiles = columns // LANES
     scale_rows = (capacity * tiles + 15) // 16 * 16
     rows = capacity * columns + scale_rows
+    scalars = pl.BlockSpec(memory_space=pltpu.SMEM)
     landed = pl.pallas_call(
         functools.partial(exchange_kernel, shards, capacity),
         out_shape=jax.ShapeDtypeStruct((cores, shards, rows, LANES), jnp.bfloat16),
-        in_specs=[pl.BlockSpec(memory_space=pltpu.SMEM), pl.BlockSpec(memory_space=pltpu.VMEM)],
+        in_specs=[scalars, scalars, pl.BlockSpec(memory_space=pl.ANY)],
         out_specs=pl.BlockSpec(memory_space=pl.ANY),
         scratch_shapes=[
+            pltpu.VMEM(weights.shape, jnp.bfloat16),
             pltpu.VMEM((shards, rows, LANES), jnp.bfloat16),
+            pltpu.SMEM((per_device,), jnp.int32),
+            pltpu.SemaphoreType.DMA,
             pltpu.SemaphoreType.DMA((shards,)),
             pltpu.SemaphoreType.DMA((shards,)),
             pltpu.SemaphoreType.DMA((shards,)),
@@ -228,23 +282,27 @@
             collective_id=0, has_side_effects=True, vmem_limit_bytes=48 * 1024 * 1024
         ),
         name="exchange",
-    )(source, weights)
+    )(block_ids, owner_map, weights)
     return pl.pallas_call(
         functools.partial(place_kernel, capacity, columns),
         out_shape=(
             jax.ShapeDtypeStruct((1, cores * columns, per_device * height), jnp.bfloat16),
             jax.ShapeDtypeStruct((1, cores * tiles, per_device), jnp.bfloat16),
         ),
-        in_specs=[pl.BlockSpec(memory_space=pltpu.SMEM), pl.BlockSpec(memory_space=pl.ANY)],
+        in_specs=[scalars, scalars, pl.BlockSpec(memory_space=pl.ANY)],
         out_specs=(pl.BlockSpec(memory_space=pl.ANY), pl.BlockSpec(memory_space=pltpu.VMEM)),
         scratch_shapes=[
+            pltpu.VMEM((cores * tiles, shards, capacity * LANES, LANES), jnp.bfloat16),
+            pltpu.VMEM((cores * tiles, LANES, per_device * height), jnp.bfloat16),
             pltpu.VMEM((cores, shards, scale_rows, LANES), jnp.bfloat16),
+            pltpu.SMEM((per_device + 1,), jnp.int32),
+            pltpu.SemaphoreType.DMA((cores * tiles,)),
+            pltpu.SemaphoreType.DMA((cores * tiles,)),
             pltpu.SemaphoreType.DMA,
-            pltpu.SemaphoreType.DMA((cores, per_device)),
         ],
         compiler_params=pltpu.CompilerParams(vmem_limit_bytes=48 * 1024 * 1024),
         name="place",
-    )(picking, landed)
+    )(block_ids, owner_map, landed)
 
 
 def solution(mesh):

time: 334 us -> 112 us (0.34)
  Pallas kernels: 325 us -> 108 us
  other arithmetic: 4.31 us -> 0 us
    pallas_call x1, Pallas kernels: 225 us -> 7.74 us  [body(): pl.pallas_call(functools.partial(place_kernel, capacity, columns), out_sh...]
    reduce_sum x6 -> x0, other arithmetic: 3.55 us -> none  [the longest x1 1.29 us: body(): my_expert = jnp.sum(jnp.where(owner_map == myself, expert_ids, 0))]
where the time goes in v2:
time: 112 us
  Pallas kernels  108 us (96%)
  local copies, waits for them, and re-layouts  3.36 us (3%)
    pallas_call x1, Pallas kernels, body(): pl.pallas_call(functools.partial(exchange_kernel, shards, capacity), out_...  101 us
    pallas_call x1, Pallas kernels, body(): pl.pallas_call(functools.partial(place_kernel, capacity, columns), out_sh...  7.74 us
    unnamed x6, local copies, waits for them, and re-layouts  3.36 us

profile of v2, /device:TPU:11, one launch (start us, length us, event | category | flops | bytes accessed | tf_op | source)
XLA Modules:
  0.0 112.3 jit_solution(3034108879484578639)
XLA Ops:
  0.6 0.0 copy-start
  0.6 2.0 %copy-done = bf16[28,128,512]{2,1,0:T(8,128)(2,1)S(1)} copy-done((bf16[28,128,512]{2,1,0:T(8,128)(2,1)S(1)}, bf16[28,128,512]{2,1,0:T(8,128)(2,1)}, u32[]{:S(2)}) %copy-start) | copy-done | bytes 3670040
  2.7 0.0 copy-start.1
  2.7 0.7 copy-done.1
  3.3 0.0 copy-start.2
  3.4 0.7 copy-done.2
  4.0 100.5 %exchange.1.landed_ref = bf16[2,8,2064,128]{3,2,1,0:T(8,128)(2,1)} custom-call(s32[224]{0:T(256)S(1)} %copy-done.1, s32[8]{0:T(128)S(1)} %copy-done.2, bf16[28,128,512]{2,1,0:T(8,128)(2,1)S(1)} %copy-done), custom_call_target="tpu_custom_call" | custom-call | tf_op jit(solution)/shard_map/exchange/pallas_call | solution.py:266
  104.5 7.7 %place.1 = (bf16[1,1024,3584]{2,1,0:T(8,128)(2,1)}, bf16[1,8,28]{2,1,0:T(8,128)(2,1)}) custom-call(s32[224]{0:T(256)S(1)} %copy-done.1, s32[8]{0:T(128)S(1)} %copy-done.2, bf16[2,8,2064,128]{3,2,1,0:T(8,128)(2,1)} %exchange.1.landed_ref), custom_call_target="tpu_custom_call" | custom-call | tf_op jit(solution)/shard_map/place/pallas_call | solution.py:286
Async XLA Ops:
  0.6 2.0 %copy-start = (bf16[28,128,512]{2,1,0:T(8,128)(2,1)S(1)}, bf16[28,128,512]{2,1,0:T(8,128)(2,1)}, u32[]{:S(2)}) copy-start(bf16[28,128,512]{2,1,0:T(8,128)(2,1)} %weights_ref.1) | copy-start | bytes 11010052
  2.7 0.7 copy-start.1
  3.3 0.7 copy-start.2

commit v3 on v2

v3 whole, which is shorter than its diff:
```python
import functools

import jax
import jax.numpy as jnp
from jax import lax
from jax.experimental import pallas as pl
from jax.experimental.pallas import tpu as pltpu
from jax.sharding import PartitionSpec as P

MESH = pl.DeviceIdType.MESH
LANES = 128


def far_first(step, shards):
    distance = (step + 1) // 2
    sign = 1 - 2 * ((step + 1) % 2)
    return (shards // 2 + sign * distance + shards) % shards


def exchange_kernel(
    shards,
    capacity,
    block_ids_ref,
    owner_map_ref,
    weights_ref,
    landed_ref,
    landed_scales_ref,
    held_weights,
    outgoing,
    outgoing_scales,
    owner_of,
    read_sem,
    send_sem,
    recv_sem,
    pass_sem,
    passed_sem,
):
    me = lax.axis_index("fsdp")
    core = lax.axis_index("rep")
    other = 1 - core
    per_device, _, columns = weights_ref.shape
    tiles = columns // LANES
    read = pltpu.make_async_copy(weights_ref, held_weights, read_sem)
    read.start()

    barrier = pltpu.get_barrier_semaphore()

    def greet(step, carry):
        peer = (me + step) % shards
        pl.semaphore_signal(barrier, inc=1, device_id={"fsdp": peer}, device_id_type=MESH)
        return carry

    lax.fori_loop(1, shards, greet, 0)
    pl.semaphore_signal(barrier, inc=1, device_id={"rep": other}, device_id_type=MESH)

    def look_up(index, carry):
        owner_of[index] = owner_map_ref[lax.div(block_ids_ref[me * per_device + index], per_device)]
        return carry

    lax.fori_loop(0, per_device, look_up, 0)
    pl.semaphore_wait(barrier, shards)
    read.wait()

    def sources_for(owner):
        def step(index, carry):
            count, found = carry
            hit = owner_of[index] == owner
            found = tuple(jnp.where(hit & (count == slot), index, old) for slot, old in enumerate(found))
            return count + hit.astype(jnp.int32), found

        zero = jnp.int32(0)
        return lax.fori_loop(0, per_device, step, (zero, (zero,) * capacity))[1]

    def fill(owner, slot, source, scale_tile):
        row_ids = lax.broadcasted_iota(jnp.int32, scale_tile.shape, 0)
        for tile in range(tiles):
            block = held_weights[source, :, tile * LANES : (tile + 1) * LANES].astype(jnp.float32)
            largest = jnp.max(jnp.max(jnp.abs(block), axis=0, keepdims=True), axis=1, keepdims=True)
            scale = (largest + 1e-06).astype(jnp.bfloat16).astype(jnp.float32)
            divided = (block / scale).astype(jnp.bfloat16)
            outgoing[owner, slot, tile * LANES : (tile + 1) * LANES, :] = divided.T
            scale_tile = jnp.where(row_ids == slot * tiles + tile, scale, scale_tile)
        return scale_tile

    def copy(start, landing, part, device, done, arrived):
        if part < capacity:
            start_ref, landing_ref = start[0].at[start[2], part], landing[0].at[landing[2], landing[3], part]
        else:
            start_ref, landing_ref = start[1].at[start[2]], landing[1].at[landing[2], landing[3]]
        return pltpu.make_async_remote_copy(
            src_ref=start_ref,
            dst_ref=landing_ref,
            send_sem=done,
            recv_sem=arrived,
            device_id=device,
            device_id_type=MESH,
        )

    outbox = (outgoing, outgoing_scales)
    landed = (landed_ref, landed_scales_ref)

    def to_owner(owner, part):
        return copy(
            (*outbox, owner), (*landed, core, me), part, {"fsdp": owner}, send_sem.at[owner, part], recv_sem.at[me, part]
        )

    def from_sender(sender, part):
        return copy(
            (*outbox, sender),
            (*landed, core, sender),
            part,
            {"fsdp": sender},
            send_sem.at[sender, part],
            recv_sem.at[sender, part],
        )

    def between_cores(half, sender, part):
        here = (landed_ref.at[half], landed_scales_ref.at[half], sender)
        return copy(
            here,
            (*landed, half, sender),
            part,
            {"rep": other},
            pass_sem.at[sender, part],
            passed_sem.at[sender, part],
        )

    def keep(part):
        if part < capacity:
            start_ref, landing_ref = outgoing.at[me, part], landed_ref.at[core, me, part]
        else:
            start_ref, landing_ref = outgoing_scales.at[me], landed_scales_ref.at[core, me]
        return pltpu.make_async_copy(start_ref, landing_ref, recv_sem.at[me, part])

    def prepare(owner, launch):
        sources = sources_for(owner)
        scale_tile = jnp.zeros(outgoing_scales.shape[1:], jnp.float32)
        for slot in range(capacity):
            scale_tile = fill(owner, slot, sources[slot], scale_tile)
            launch(slot).start()
        outgoing_scales[owner] = scale_tile.astype(jnp.bfloat16)
        launch(capacity).start()

    parts = range(capacity + 1)

    def send(step, carry):
        owner = (me + far_first(step, shards)) % shards
        prepare(owner, functools.partial(to_owner, owner))
        return carry

    lax.fori_loop(0, shards - 1, send, 0)
    prepare(me, keep)
    for part in parts:
        keep(part).wait()
        between_cores(core, me, part).start()

    def forward(step, carry):
        sender = (me - far_first(step, shards) + shards) % shards
        for part in parts:
            from_sender(sender, part).wait_recv()
            between_cores(core, sender, part).start()
        return carry

    lax.fori_loop(0, shards - 1, forward, 0)

    def finish(step, carry):
        peer = (me + step) % shards
        for part in parts:
            to_owner(peer, part).wait_send()
        return carry

    lax.fori_loop(1, shards, finish, 0)

    def finish_core(sender, carry):
        for part in parts:
            between_cores(core, sender, part).wait_send()
            between_cores(other, sender, part).wait_recv()
        return carry

    lax.fori_loop(0, shards, finish_core, 0)


def place_kernel(
    block_ids_ref,
    owner_map_ref,
    landed_ref,
    landed_scales_ref,
    matrix_ref,
    scales_ref,
    pieces,
    staged,
    scale_tiles,
    pick_ref,
    read_sems,
    write_sems,
    scale_sem,
):
    me = lax.axis_index("fsdp")
    cores, shards, capacity, columns, _ = landed_ref.shape
    scale_rows = landed_scales_ref.shape[2]
    per_device = pick_ref.shape[0] - 1
    tiles = columns // LANES

    def read(piece):
        half, tile = piece // tiles, piece % tiles
        return pltpu.make_async_copy(
            landed_ref.at[half, :, :, pl.ds(tile * LANES, LANES), :], pieces.at[piece], read_sems.at[piece]
        )

    def write(piece):
        return pltpu.make_async_copy(
            staged.at[piece], matrix_ref.at[0, pl.ds(piece * LANES, LANES), :], write_sems.at[piece]
        )

    scale_copy = pltpu.make_async_copy(landed_scales_ref, scale_tiles, scale_sem)
    for piece in range(cores * tiles):
        read(piece).start()
    scale_copy.start()

    def find_expert(expert, found):
        return jnp.where(owner_map_ref[expert] == me, expert, found)

    lowest = per_device * lax.fori_loop(0, owner_map_ref.shape[0], find_expert, jnp.int32(0))

    def look_up(sender, carry):
        count = jnp.int32(0)
        for index in range(per_device):
            row = block_ids_ref[sender * per_device + index] - lowest
            hit = (row >= 0) & (row < per_device)
            pick_ref[jnp.where(hit, row, per_device)] = sender * capacity + count
            count = count + hit.astype(jnp.int32)
        return carry

    lax.fori_loop(0, shards, look_up, 0)

    for piece in range(cores * tiles):
        read(piece).wait()

        for index in range(per_device):
            picked = pick_ref[index]
            sender, slot = lax.div(picked, capacity), lax.rem(picked, capacity)
            staged[piece, :, index * LANES : (index + 1) * LANES] = pieces[piece, sender, slot]
        write(piece).start()
    scale_copy.wait()
    lanes = lax.broadcasted_iota(jnp.int32, (scale_rows, LANES), 1)
    rows_of = lax.broadcasted_iota(jnp.int32, (scale_rows, LANES), 0)

    def gather(index, totals):
        picked = pick_ref[index]
        sender, slot = lax.div(picked, capacity), lax.rem(picked, capacity)
        hit = (lanes == index) & (rows_of // tiles == slot)
        return tuple(
            jnp.where(hit, scale_tiles[half, sender].astype(jnp.float32), totals[half]) for half in range(cores)
        )

    zero = jnp.zeros((scale_rows, LANES), jnp.float32)
    totals = lax.fori_loop(0, per_device, gather, (zero,) * cores)
    for half in range(cores):
        folded = jnp.zeros((tiles, LANES), jnp.float32)
        for slot in range(capacity):
            folded = folded + totals[half][slot * tiles : (slot + 1) * tiles]
        scales_ref[0, half * tiles : (half + 1) * tiles, :] = folded[:, :per_device].astype(jnp.bfloat16)

    for piece in range(cores * tiles):
        write(piece).wait()


def body(weights, block_ids, owner_map):
    shards = lax.axis_size("fsdp")
    cores = lax.axis_size("rep")
    per_device, height, columns = weights.shape
    capacity = (per_device + shards - 1) // shards
    tiles = columns // LANES
    scale_rows = (capacity * tiles + 15) // 16 * 16
    scalars = pl.BlockSpec(memory_space=pltpu.SMEM)
    anywhere = pl.BlockSpec(memory_space=pl.ANY)
    landed, landed_scales = pl.pallas_call(
        functools.partial(exchange_kernel, shards, capacity),
        out_shape=(
            jax.ShapeDtypeStruct((cores, shards, capacity, columns, LANES), jnp.bfloat16),
            jax.ShapeDtypeStruct((cores, shards, scale_rows, LANES), jnp.bfloat16),
        ),
        in_specs=[scalars, scalars, anywhere],
        out_specs=(anywhere, anywhere),
        scratch_shapes=[
            pltpu.VMEM(weights.shape, jnp.bfloat16),
            pltpu.VMEM((shards, capacity, columns, LANES), jnp.bfloat16),
            pltpu.VMEM((shards, scale_rows, LANES), jnp.bfloat16),
            pltpu.SMEM((per_device,), jnp.int32),
            pltpu.SemaphoreType.DMA,
            pltpu.SemaphoreType.DMA((shards, capacity + 1)),
            pltpu.SemaphoreType.DMA((shards, capacity + 1)),
            pltpu.SemaphoreType.DMA((shards, capacity + 1)),
            pltpu.SemaphoreType.DMA((shards, capacity + 1)),
        ],
        compiler_params=pltpu.CompilerParams(
            collective_id=0, has_side_effects=True, vmem_limit_bytes=60 * 1024 * 1024
        ),
        name="exchange",
    )(block_ids, owner_map, weights)
    return pl.pallas_call(
        place_kernel,
        out_shape=(
            jax.ShapeDtypeStruct((1, cores * columns, per_device * height), jnp.bfloat16),
            jax.ShapeDtypeStruct((1, cores * tiles, per_device), jnp.bfloat16),
        ),
        in_specs=[scalars, scalars, anywhere, anywhere],
        out_specs=(anywhere, pl.BlockSpec(memory_space=pltpu.VMEM)),
        scratch_shapes=[
            pltpu.VMEM((cores * tiles, shards, capacity, LANES, LANES), jnp.bfloat16),
            pltpu.VMEM((cores * tiles, LANES, per_device * height), jnp.bfloat16),
            pltpu.VMEM((cores, shards, scale_rows, LANES), jnp.bfloat16),
            pltpu.SMEM((per_device + 1,), jnp.int32),
            pltpu.SemaphoreType.DMA((cores * tiles,)),
            pltpu.SemaphoreType.DMA((cores * tiles,)),
            pltpu.SemaphoreType.DMA,
        ],
        compiler_params=pltpu.CompilerParams(vmem_limit_bytes=60 * 1024 * 1024),
        name="place",
    )(block_ids, owner_map, landed, landed_scales)


def solution(mesh):
    return jax.shard_map(
        body,
        mesh=mesh,
        in_specs=(P(("groups", "fsdp"), None, "rep"), P(), P()),
        out_specs=(P(("groups", "fsdp"), None, None), P(("groups", "fsdp"), None, None)),
        check_vma=False,
    )
```

time: 112 us -> 110 us (0.982)
  local copies, waits for them, and re-layouts: 3.36 us -> 0 us
    unnamed x6 -> x0, local copies, waits for them, and re-layouts: 3.36 us -> none
where the time goes in v3:
time: 110 us
  Pallas kernels  109 us (99%)
    pallas_call x1, Pallas kernels, body(): pl.pallas_call(functools.partial(exchange_kernel, shards, capacity), out_...  102 us
    pallas_call x1, Pallas kernels, body(): pl.pallas_call(place_kernel, out_shape=(jax.ShapeDtypeStruct((1, cores *...  7.85 us

profile of v3, /device:TPU:11, one launch (start us, length us, event | category | flops | bytes accessed | tf_op | source)
XLA Modules:
  0.0 110.0 jit_solution(16183451053676948291)
XLA Ops:
  0.6 101.5 %exchange.1 = (bf16[2,8,4,512,128]{4,3,2,1,0:T(8,128)(2,1)}, bf16[2,8,16,128]{3,2,1,0:T(8,128)(2,1)}) custom-call(s32[224]{0:T(256)} %block_ids_ref.3, s32[8]{0:T(128)} %owner_map_ref.3, bf16[28,128,512]{2,1,0:T(8,128)(2,1)} %weights_ref.1), custom_call_target="tpu_custom_call" | custom-call | tf_op jit(solution)/shard_map/exchange/pallas_call | solution.py:277
  102.2 7.8 %place.1 = (bf16[1,1024,3584]{2,1,0:T(8,128)(2,1)}, bf16[1,8,28]{2,1,0:T(8,128)(2,1)}) custom-call(s32[224]{0:T(256)} %block_ids_ref.3, s32[8]{0:T(128)} %owner_map_ref.3, bf16[2,8,4,512,128]{4,3,2,1,0:T(8,128)(2,1)} %get-tuple-element.4.landed_ref, bf16[2,8,16,128]{3,2,1,0:T(8,128)(2,1)} %get-tuple-element.5.landed_scales_ref), custom_call_target="tpu_custom_call" | custom-call | tf_op jit(solution)/shard_map/place/pallas_call | solution.py:301

commit v4 on v3

--- a/solution.py
+++ b/solution.py
@@ -214,7 +214,7 @@
 
     scale_copy = pltpu.make_async_copy(landed_scales_ref, scale_tiles, scale_sem)
     for piece in range(cores * tiles):
-        read(piece).start()
+        read(piece).start(priority=piece % 2)
     scale_copy.start()
 
     def find_expert(expert, found):
@@ -240,7 +240,7 @@
             picked = pick_ref[index]
             sender, slot = lax.div(picked, capacity), lax.rem(picked, capacity)
             staged[piece, :, index * LANES : (index + 1) * LANES] = pieces[piece, sender, slot]
-        write(piece).start()
+        write(piece).start(priority=1)
     scale_copy.wait()
     lanes = lax.broadcasted_iota(jnp.int32, (scale_rows, LANES), 1)
     rows_of = lax.broadcasted_iota(jnp.int32, (scale_rows, LANES), 0)

time: 110 us -> 110 us (level)
  no operation moved by 1% of the time
where the time goes in v4:
time: 110 us; the launch traced here: 109 us
  Pallas kernels  109 us (99%)
    pallas_call x1, Pallas kernels, body(): pl.pallas_call(functools.partial(exchange_kernel, shards, capacity), out_...  102 us
    pallas_call x1, Pallas kernels, body(): pl.pallas_call(place_kernel, out_shape=(jax.ShapeDtypeStruct((1, cores *...  7.19 us

profile of v4, /device:TPU:11, one launch (start us, length us, event | category | flops | bytes accessed | tf_op | source)
XLA Modules:
  0.0 109.4 jit_solution(17046461150659054320)
XLA Ops:
  0.6 101.5 %exchange.1 = (bf16[2,8,4,512,128]{4,3,2,1,0:T(8,128)(2,1)}, bf16[2,8,16,128]{3,2,1,0:T(8,128)(2,1)}) custom-call(s32[224]{0:T(256)} %block_ids_ref.3, s32[8]{0:T(128)} %owner_map_ref.3, bf16[28,128,512]{2,1,0:T(8,128)(2,1)} %weights_ref.1), custom_call_target="tpu_custom_call" | custom-call | tf_op jit(solution)/shard_map/exchange/pallas_call | solution.py:277
  102.2 7.2 %place.1 = (bf16[1,1024,3584]{2,1,0:T(8,128)(2,1)}, bf16[1,8,28]{2,1,0:T(8,128)(2,1)}) custom-call(s32[224]{0:T(256)} %block_ids_ref.3, s32[8]{0:T(128)} %owner_map_ref.3, bf16[2,8,4,512,128]{4,3,2,1,0:T(8,128)(2,1)} %get-tuple-element.4.landed_ref, bf16[2,8,16,128]{3,2,1,0:T(8,128)(2,1)} %get-tuple-element.5.landed_scales_ref), custom_call_target="tpu_custom_call" | custom-call | tf_op jit(solution)/shard_map/place/pallas_call | solution.py:301

commit v5 on v4

--- a/solution.py
+++ b/solution.py
@@ -40,8 +40,13 @@
     other = 1 - core
     per_device, _, columns = weights_ref.shape
     tiles = columns // LANES
-    read = pltpu.make_async_copy(weights_ref, held_weights, read_sem)
-    read.start()
+    middle = per_device // 2
+    reads = [
+        pltpu.make_async_copy(weights_ref.at[part], held_weights.at[part], read_sem.at[queue])
+        for queue, part in enumerate((pl.ds(0, middle), pl.ds(middle, per_device - middle)))
+    ]
+    for queue, read in enumerate(reads):
+        read.start(priority=queue)
 
     barrier = pltpu.get_barrier_semaphore()
 
@@ -59,7 +64,8 @@
 
     lax.fori_loop(0, per_device, look_up, 0)
     pl.semaphore_wait(barrier, shards)
-    read.wait()
+    for read in reads:
+        read.wait()
 
     def sources_for(owner):
         def step(index, carry):
@@ -201,10 +207,13 @@
     per_device = pick_ref.shape[0] - 1
     tiles = columns // LANES
 
-    def read(piece):
+    def read(piece, queue):
+        senders = pl.ds(queue * (shards // 2), shards // 2)
         half, tile = piece // tiles, piece % tiles
         return pltpu.make_async_copy(
-            landed_ref.at[half, :, :, pl.ds(tile * LANES, LANES), :], pieces.at[piece], read_sems.at[piece]
+            landed_ref.at[half, senders, :, pl.ds(tile * LANES, LANES), :],
+            pieces.at[piece, senders],
+            read_sems.at[piece, queue],
         )
 
     def write(piece):
@@ -214,7 +223,8 @@
 
     scale_copy = pltpu.make_async_copy(landed_scales_ref, scale_tiles, scale_sem)
     for piece in range(cores * tiles):
-        read(piece).start(priority=piece % 2)
+        for queue in range(2):
+            read(piece, queue).start(priority=queue)
     scale_copy.start()
 
     def find_expert(expert, found):
@@ -234,7 +244,8 @@
     lax.fori_loop(0, shards, look_up, 0)
 
     for piece in range(cores * tiles):
-        read(piece).wait()
+        for queue in range(2):
+            read(piece, queue).wait()
 
         for index in range(per_device):
             picked = pick_ref[index]
@@ -287,7 +298,7 @@
             pltpu.VMEM((shards, capacity, columns, LANES), jnp.bfloat16),
             pltpu.VMEM((shards, scale_rows, LANES), jnp.bfloat16),
             pltpu.SMEM((per_device,), jnp.int32),
-            pltpu.SemaphoreType.DMA,
+            pltpu.SemaphoreType.DMA((2,)),
             pltpu.SemaphoreType.DMA((shards, capacity + 1)),
             pltpu.SemaphoreType.DMA((shards, capacity + 1)),
             pltpu.SemaphoreType.DMA((shards, capacity + 1)),
@@ -311,7 +322,7 @@
             pltpu.VMEM((cores * tiles, LANES, per_device * height), jnp.bfloat16),
             pltpu.VMEM((cores, shards, scale_rows, LANES), jnp.bfloat16),
             pltpu.SMEM((per_device + 1,), jnp.int32),
-            pltpu.SemaphoreType.DMA((cores * tiles,)),
+            pltpu.SemaphoreType.DMA((cores * tiles, 2)),
             pltpu.SemaphoreType.DMA((cores * tiles,)),
             pltpu.SemaphoreType.DMA,
         ],

time: 110 us -> 109 us (level)
  no operation moved by 1% of the time
where the time goes in v5:
time: 109 us
  Pallas kernels  109 us (100%)
    pallas_call x1, Pallas kernels, body(): pl.pallas_call(functools.partial(exchange_kernel, shards, capacity), out_...  102 us
    pallas_call x1, Pallas kernels, body(): pl.pallas_call(place_kernel, out_shape=(jax.ShapeDtypeStruct((1, cores *...  7.04 us

profile of v5, /device:TPU:11, one launch (start us, length us, event | category | flops | bytes accessed | tf_op | source)
XLA Modules:
  0.0 109.2 jit_solution(3513638229737682472)
XLA Ops:
  0.6 101.6 %exchange.1 = (bf16[2,8,4,512,128]{4,3,2,1,0:T(8,128)(2,1)}, bf16[2,8,16,128]{3,2,1,0:T(8,128)(2,1)}) custom-call(s32[224]{0:T(256)} %block_ids_ref.3, s32[8]{0:T(128)} %owner_map_ref.3, bf16[28,128,512]{2,1,0:T(8,128)(2,1)} %weights_ref.1), custom_call_target="tpu_custom_call" | custom-call | tf_op jit(solution)/shard_map/exchange/pallas_call | solution.py:288
  102.2 7.0 %place.1 = (bf16[1,1024,3584]{2,1,0:T(8,128)(2,1)}, bf16[1,8,28]{2,1,0:T(8,128)(2,1)}) custom-call(s32[224]{0:T(256)} %block_ids_ref.3, s32[8]{0:T(128)} %owner_map_ref.3, bf16[2,8,4,512,128]{4,3,2,1,0:T(8,128)(2,1)} %get-tuple-element.4.landed_ref, bf16[2,8,16,128]{3,2,1,0:T(8,128)(2,1)} %get-tuple-element.5.landed_scales_ref), custom_call_target="tpu_custom_call" | custom-call | tf_op jit(solution)/shard_map/place/pallas_call | solution.py:312
